TPU v7x, 512 devices: a whole 4x4x16 slice. The times are simulated.
512 devices in a mesh: row: 16 (over y, x_lo, core), loop: 32 (over x_hi, z).
Axes of the slice: x: 4 (x_hi: 2, x_lo: 2; x = x_hi * 2 + x_lo), y: 4, z: 16, core: 2. Of those that a mesh axis runs over, the one named last changes fastest.
Arguments:
- gradient: bfloat16 [8192, 28672], P('row', 'loop'), may hold values from -6 to 6
- left_basis: bfloat16 [8192, 512], P('row'), may hold values from -0.0625 to 0.0625
- right_basis: bfloat16 [28672, 8192], P('loop', 'row'), may hold values from -0.03125 to 0.03125
- first_moment: float32 [512, 8192], P('loop', 'row'), may hold values from -6 to 6
- second_moment: float32 [512, 8192], P('loop', 'row'), may hold values from 0.25 to 4
Outputs:
- update: bfloat16 [8192, 28672], P('row', 'loop')
- first_next: float32 [512, 8192], P('loop', 'row')
- second_next: float32 [512, 8192], P('loop', 'row')
All inputs are finite; a program needn't handle non-finite values.
Results may differ from a plain program's by a relative error of at most 0.0075.
Values may be sent and summed in bfloat16 or wider, within the bound.
A program may use at most 64 MiB of HBM per device.

v0:
```python
import jax
import jax.numpy as jnp
from jax import lax
from jax.sharding import PartitionSpec as P


def per_device(gradient, left_basis, right_basis, first_moment, second_moment):
    partial_value = jnp.einsum(
        "dr,dn->rn", left_basis, gradient, preferred_element_type=jnp.float32
    )
    rotated_half = lax.psum(partial_value, "row").astype(jnp.bfloat16)
    projected = lax.psum_scatter(
        jnp.dot(rotated_half, right_basis, preferred_element_type=jnp.float32),
        "loop",
        scatter_dimension=0,
        tiled=True,
    )
    first_next = 0.9 * first_moment + 0.1 * projected
    second_next = 0.95 * second_moment + 0.05 * projected * projected
    direction = (first_next / (jnp.sqrt(second_next) + 1e-08)).astype(jnp.bfloat16)
    every_row = lax.all_gather(direction, "loop", axis=0, tiled=True)
    back_part = jnp.einsum("rc,nc->rn", every_row, right_basis, preferred_element_type=jnp.float32)
    back = lax.psum(back_part, "row").astype(jnp.bfloat16)
    update = jnp.dot(left_basis, back, preferred_element_type=jnp.float32).astype(jnp.bfloat16)
    return (update, first_next, second_next)


def solution(mesh):
    placed = (
        P("row", "loop"),
        P("row", None),
        P("loop", "row"),
        P("loop", "row"),
        P("loop", "row"),
    )
    return jax.shard_map(
        per_device,
        mesh=mesh,
        in_specs=placed,
        out_specs=(P("row", "loop"), P("loop", "row"), P("loop", "row")),
        check_vma=False,
    )
```

profile of v0, /device:TPU:1, one launch (start us, length us, event | category | flops | bytes accessed | tf_op | source)
XLA Modules:
  0.0 883.3 jit_solution(12267969522693044865)
XLA Ops:
  7.2 0.0 copy-start
  7.2 0.0 reduce-scatter.2.cloned.1.call-start
  7.2 2.1 fusion.6
  9.4 72.8 %all-reduce.2 = bf16[512,896]{1,0:T(8,128)(2,1)} all-reduce(f32[512,896]{1,0:T(8,128)S(1)} %fusion.6), channel_id=1, replica_groups=mesh['row'=16,'loop'=32] {'row'}, use_global_device_ids=true, to_apply=%region_0.0 | all-reduce | flops 458752 | bytes 2752512 | tf_op jit(solution)/shard_map/psum | solution.py:11
  82.2 0.0 copy-done
  82.2 0.0 copy-start.2
  82.2 0.0 copy-start.3
  82.2 2.9 fusion.8
  85.1 0.0 reduce-scatter.2.cloned.1.call-update
  85.1 631.6 %reduce-scatter.2.cloned.1.call-done = f32[16,512]{1,0:T(8,128)} async-done(((f32[512,512]{1,0:T(8,128)}), f32[16,512]{1,0:T(8,128)}) %reduce-scatter.2.cloned.1.call-update) | async-done | bytes 32784 | tf_op jit(solution)/shard_map/reduce_scatter | solution.py:12
  716.7 0.0 copy-done.2
  716.7 0.0 copy-done.3
  716.7 1.4 divide_convert_fusion
  718.1 61.6 %all_gather.3 = bf16[512,512]{1,0:T(8,128)(2,1)S(1)} all-gather(bf16[16,512]{1,0:T(8,128)(2,1)S(1)} %get-tuple-element.6), channel_id=1, replica_groups=mesh['row'=16,'loop'=32] {'loop'}, dimensions={0}, use_global_device_ids=true | all-gather | bytes 540672 | tf_op jit(solution)/shard_map/all_gather | solution.py:21
  779.7 0.7 fusion.7
  780.4 0.0 copy-start.1
  780.5 92.9 %all-reduce.3 = bf16[512,896]{1,0:T(8,128)(2,1)} all-reduce(f32[512,896]{1,0:T(8,128)S(1)} %fusion.7), channel_id=1, replica_groups=mesh['row'=16,'loop'=32] {'row'}, use_global_device_ids=true, to_apply=%region_2.0 | all-reduce | flops 458752 | bytes 2752512 | tf_op jit(solution)/shard_map/psum | solution.py:23
  873.3 0.0 copy-done.1
  873.3 1.9 fusion
  875.2 1.3 copy.8
Async XLA Ops:
  7.2 75.0 %copy-start = (bf16[896,512]{1,0:T(8,128)(2,1)S(1)}, bf16[896,512]{1,0:T(8,128)(2,1)}, u32[]{:S(2)}) copy-start(bf16[896,512]{1,0:T(8,128)(2,1)} %param.7) | copy-start | bytes 2752516
  7.2 709.5 %reduce-scatter.2.cloned.1.call-start = ((), (), s32[]{:S(2)}) async-start(), calls=%async_computation.1 | async-start | bytes 1081344 | tf_op jit(solution)/shard_map/reduce_scatter | solution.py:12
  82.2 634.5 %copy-start.2 = (f32[16,512]{1,0:T(8,128)S(1)}, f32[16,512]{1,0:T(8,128)}, u32[]{:S(2)}) copy-start(f32[16,512]{1,0:T(8,128)} %param.9) | copy-start | bytes 98308
  82.2 634.5 %copy-start.3 = (f32[16,512]{1,0:T(8,128)S(1)}, f32[16,512]{1,0:T(8,128)}, u32[]{:S(2)}) copy-start(f32[16,512]{1,0:T(8,128)} %param.8) | copy-start | bytes 98308
  780.4 92.9 %copy-start.1 = (bf16[512,512]{1,0:T(8,128)(2,1)S(1)}, bf16[512,512]{1,0:T(8,128)(2,1)}, u32[]{:S(2)}) copy-start(bf16[512,512]{1,0:T(8,128)(2,1)} %param.6) | copy-start | bytes 1572868
Sparse Core Ops, SparseCore 0:
  85.2 631.4 reduce-scatter.1
where the time goes:
time: 885 us; the launch traced here: 883 us
  waiting for transfers between devices  632 us (71%)
  blocking collectives  227 us (26%)
  between operations  14.1 us (2%)
    reduce_scatter x1, waiting for transfers between devices, per_device(): lax.psum_scatter(jnp.dot(rotated_half, right_basis, preferred_element_typ...  632 us
    psum x1, blocking collectives, per_device(): back = lax.psum(back_part, 'row').astype(jnp.bfloat16)  92.9 us
    psum x1, blocking collectives, per_device(): rotated_half = lax.psum(partial_value, 'row').astype(jnp.bfloat16)  72.8 us
    all_gather x1, blocking collectives, per_device(): every_row = lax.all_gather(direction, 'loop', axis=0, tiled=True)  61.6 us
  transfers between devices with their start and end apart: 1, of which 1 were waited for; matrix products, arithmetic and copies ran while one was open for 0% of the time, Pallas kernels for 0%

commit v1 on v0

v1 whole, which is shorter than its diff:
```python
import functools

import jax
import jax.numpy as jnp
from jax import lax
from jax.experimental import pallas as pl
from jax.experimental.pallas import tpu as pltpu
from jax.sharding import PartitionSpec as P

MESH = pl.DeviceIdType.MESH
BF16 = jnp.bfloat16
F32 = jnp.float32
RING = 16
QUAD = 4


def dot(a, b):
    return jnp.dot(a, b, preferred_element_type=F32)


def kernel(
    g_hbm, l_hbm, q_hbm, m1_ref, m2_ref,
    update_ref, first_ref, second_ref,
    g, lb, q, lt, qt,
    xs, xr, hs, rr, keep, full,
    ps, own, bq, bs, br, dirp, dirf,
    in_sem, core_s, core_r, sum_s, sum_r, all_s, all_r, relay_s, relay_r,
    near_s, near_r, far_s, far_r, dfar_s, dfar_r, dnear_s, dnear_r,
):
    row, loop = lax.axis_index("row"), lax.axis_index("loop")
    core, x, y = row % 2, (row // 2) % 2, row // 4
    xh, z = loop // RING, loop % RING
    chip = y * 2 + x
    sign = 1 - 2 * core

    loads = [
        pltpu.make_async_copy(src, dst, in_sem.at[n])
        for n, (src, dst) in enumerate(((l_hbm, lb), (g_hbm, g), (q_hbm, q)))
    ]
    for load in loads:
        load.start()

    sibling = (row + 1 - 2 * core, loop)

    def chip_of(m):
        py = y
        if m & 2:
            py = py + 1 - 2 * (py % 2)
        if m & 4:
            py = (py + 2) % 4
        px = 1 - x if m & 1 else x
        return py * 2 + px

    def in_row(m):
        return (chip_of(m) * 2 + core, loop)

    def in_loop(plane, offset):
        return (row, plane * RING + (z + offset + RING) % RING)

    offsets = (2 * sign, 1, -1)
    here, there = xh, 1 - xh

    barrier = pltpu.get_barrier_semaphore()
    senders = [sibling] + [in_row(m) for m in range(1, 8)]
    senders += [in_loop(plane, -o) for plane in (here, there) for o in offsets]
    senders += [in_loop(there, 0)] + [in_loop(here, QUAD * t) for t in (1, 2, 3)]
    for device in senders:
        pl.semaphore_signal(barrier, inc=1, device_id=device, device_id_type=MESH)

    loads[0].wait()
    turned = lb[...].T
    for plane in range(2):
        for a in range(QUAD):
            for s in range(QUAD):
                src, dst = plane * RING + a * QUAD + s, plane * RING + s * QUAD + a
                lt[dst * 16 : dst * 16 + 16, :] = turned[src * 16 : src * 16 + 16, :]
    loads[1].wait()

    def send(src, dst, s_sem, r_sem, device):
        copy = pltpu.make_async_remote_copy(
            src_ref=src, dst_ref=dst, send_sem=s_sem, recv_sem=r_sem,
            device_id=device, device_id_type=MESH,
        )
        copy.start()
        return copy

    sent = []

    def row_sum(turn, part, after_own, after_other):
        block = [128 * (1 - y // 2), 128 * (y // 2)]
        crossing = []
        for c in range(2):
            xs[turn, c] = part(256 * (1 - core) + block[c]).astype(BF16)
            if turn == 0 and c == 0:
                pl.semaphore_wait(barrier, 18)
            crossing.append(
                send(xs.at[turn, c], xr.at[turn, c], core_s.at[turn, c], core_r.at[turn, c], sibling)
            )
        summing = {}
        for c, relations in ((0, (5, 7, 4, 6)), (1, (3, 2, 1))):
            mine = part(256 * core + block[c])
            crossing[c].wait_recv()
            both = mine + xr[turn, c].astype(F32)
            hs[turn, c] = both.astype(BF16)
            if c == 1:
                keep[...] = both
            for m in relations:
                piece = hs.at[turn, c, pl.ds(pl.multiple_of(32 * (chip_of(m) % 4), 32), 32)]
                summing[m] = send(
                    piece, rr.at[turn, m - 1], sum_s.at[turn, m - 1], sum_r.at[turn, m - 1], in_row(m)
                )
        total = keep[pl.ds(pl.multiple_of(32 * (chip % 4), 32), 32), :]
        for m in (1, 2, 6, 4, 3, 7, 5):
            summing[m].wait_recv()
            total = total + rr[turn, m - 1].astype(F32)

        def rows(half, m):
            return pl.ds(pl.multiple_of(256 * half + 32 * chip_of(m), 32), 32)

        full[turn, rows(core, 0), :] = total.astype(BF16)
        spreading = {}
        for m in (5, 7, 3, 4, 6, 2, 1):
            piece = full.at[turn, rows(core, 0)]
            spreading[m] = send(
                piece, piece, all_s.at[turn, m - 1], all_r.at[turn, m - 1], in_row(m)
            )
        relays = []
        for m in (0, 1, 2, 6, 4, 3, 7, 5):
            piece = full.at[turn, rows(core, m)]
            if m:
                landed = pltpu.make_async_remote_copy(
                    src_ref=piece, dst_ref=piece, send_sem=all_s.at[turn, m - 1],
                    recv_sem=all_r.at[turn, m - 1], device_id=in_row(m), device_id_type=MESH,
                )
                landed.wait_recv()
            relays.append(
                send(piece, piece, relay_s.at[turn, m], relay_r.at[turn, m], sibling)
            )
        after_own()
        for m in range(8):
            piece = full.at[turn, rows(1 - core, m)]
            landed = pltpu.make_async_remote_copy(
                src_ref=piece, dst_ref=piece, send_sem=relay_s.at[turn, m],
                recv_sem=relay_r.at[turn, m], device_id=sibling, device_id_type=MESH,
            )
            landed.wait_recv()
        after_other()
        sent.extend(crossing)
        sent.extend(summing.values())
        sent.extend(spreading.values())
        sent.extend(relays)

    def project(half):
        first_row = pl.multiple_of(256 * half, 256)
        value = dot(full[0, pl.ds(first_row, 256), :], q[...])
        own[half] = value
        ps[pl.ds(first_row, 256), :] = value.astype(BF16)
        relation = (half + xh) % 2
        for t in (2, 1, 3, 0):
            for d, o in enumerate(offsets):
                zt = (z + o + RING) % RING
                at = half * RING + (zt % QUAD) * QUAD + (zt // QUAD + t) % QUAD
                slot = relation * 3 + d
                sent.append(
                    send(
                        ps.at[pl.ds(pl.multiple_of(16 * at, 16), 16)], bq.at[slot, t],
                        near_s.at[slot, t], near_r.at[slot, t], in_loop(half, o),
                    )
                )

    def project_own():
        loads[2].wait()
        project(core)

    def project_other():
        project(1 - core)
        for t in (2, 1, 3, 0):
            at = there * RING + (z % QUAD) * QUAD + (z // QUAD + t) % QUAD
            sent.append(
                send(
                    ps.at[pl.ds(pl.multiple_of(16 * at, 16), 16)], bq.at[6, t],
                    near_s.at[6, t], near_r.at[6, t], in_loop(there, 0),
                )
            )

    row_sum(
        0,
        lambda r: dot(lt[pl.ds(pl.multiple_of(r, 128), 128), :], g[...]),
        project_own,
        project_other,
    )
    qt[...] = q[...].T

    def landing(dst, s_sem, r_sem, device):
        pltpu.make_async_remote_copy(
            src_ref=dst, dst_ref=dst, send_sem=s_sem, recv_sem=r_sem,
            device_id=device, device_id_type=MESH,
        ).wait_recv()

    far = {}
    for t in (2, 1, 3, 0):
        at = (z % QUAD) * QUAD + (z // QUAD + t) % QUAD
        total = own[here, pl.ds(pl.multiple_of(16 * at, 16), 16), :]
        for slot in range(7):
            landing(bq.at[slot, t], near_s.at[slot, t], near_r.at[slot, t], sibling)
            total = total + bq[slot, t].astype(F32)
        if t:
            bs[t - 1] = total.astype(BF16)
            far[t] = send(
                bs.at[t - 1], br.at[t - 1], far_s.at[t - 1], far_r.at[t - 1], in_loop(here, QUAD * t)
            )
    for t in (1, 3, 2):
        far[t].wait_recv()
        total = total + br[t - 1].astype(F32)
    sent.extend(far.values())

    first = 0.9 * m1_ref[...] + 0.1 * total
    second = 0.95 * m2_ref[...] + 0.05 * total * total
    first_ref[...] = first
    second_ref[...] = second

    def slice_of(plane, zz):
        return pl.ds(pl.multiple_of(16 * (plane * RING + (zz % QUAD) * QUAD + zz // QUAD), 16), 16)

    def moved(o):
        return (z + o + RING) % RING

    dirp[slice_of(here, z), :] = (first / (jnp.sqrt(second) + 1e-08)).astype(BF16)

    mine = dirp.at[slice_of(here, z)]
    for t in (2, 1, 3):
        sent.append(send(mine, mine, dfar_s.at[t - 1], dfar_r.at[t - 1], in_loop(here, QUAD * t)))
    partners = [(here, o) for o in offsets] + [(there, o) for o in offsets] + [(there, 0)]
    for t in (0, 1, 3, 2):
        piece = dirp.at[slice_of(here, moved(-QUAD * t))]
        if t:
            landing(piece, dfar_s.at[t - 1], dfar_r.at[t - 1], sibling)
        for n, (plane, o) in enumerate(partners):
            sent.append(send(piece, piece, dnear_s.at[n, t], dnear_r.at[n, t], in_loop(plane, o)))
    for t in (0, 1, 3, 2):
        for n, (plane, o) in enumerate(partners):
            piece = dirp.at[slice_of(plane, moved(-o - QUAD * t))]
            landing(piece, dnear_s.at[n, t], dnear_r.at[n, t], sibling)

    for plane in range(2):
        for a in range(QUAD):
            for s in range(QUAD):
                dst, src = plane * RING + a * QUAD + s, plane * RING + s * QUAD + a
                dirf[dst * 16 : dst * 16 + 16, :] = dirp[src * 16 : src * 16 + 16, :]

    def nothing():
        pass

    row_sum(
        1,
        lambda r: dot(dirf[pl.ds(pl.multiple_of(r, 128), 128), :], qt[...]),
        nothing,
        nothing,
    )
    for c in range(4):
        update_ref[c * 128 : c * 128 + 128, :] = dot(lb[c * 128 : c * 128 + 128, :], full[1]).astype(BF16)
    for copy in sent:
        copy.wait_send()


def per_device(gradient, left_basis, right_basis, first_moment, second_moment):
    depth, width = gradient.shape
    window = left_basis.shape[1]
    cols = right_basis.shape[1]
    mine = first_moment.shape[0]
    sems = pltpu.SemaphoreType.DMA
    return pl.pallas_call(
        kernel,
        out_shape=(
            jax.ShapeDtypeStruct((depth, width), BF16),
            jax.ShapeDtypeStruct(first_moment.shape, F32),
            jax.ShapeDtypeStruct(second_moment.shape, F32),
        ),
        in_specs=[pl.BlockSpec(memory_space=pl.ANY)] * 3 + [pl.BlockSpec(memory_space=pltpu.VMEM)] * 2,
        out_specs=[pl.BlockSpec(memory_space=pltpu.VMEM)] * 3,
        scratch_shapes=[
            pltpu.VMEM((depth, width), BF16),
            pltpu.VMEM((depth, window), BF16),
            pltpu.VMEM((width, cols), BF16),
            pltpu.VMEM((window, depth), BF16),
            pltpu.VMEM((cols, width), BF16),
            pltpu.VMEM((2, 2, 128, width), BF16),
            pltpu.VMEM((2, 2, 128, width), BF16),
            pltpu.VMEM((2, 2, 128, width), BF16),
            pltpu.VMEM((2, 7, 32, width), BF16),
            pltpu.VMEM((128, width), F32),
            pltpu.VMEM((2, window, width), BF16),
            pltpu.VMEM((window, cols), BF16),
            pltpu.VMEM((2, window // 2, cols), F32),
            pltpu.VMEM((7, 4, mine, cols), BF16),
            pltpu.VMEM((3, mine, cols), BF16),
            pltpu.VMEM((3, mine, cols), BF16),
            pltpu.VMEM((window, cols), BF16),
            pltpu.VMEM((window, cols), BF16),
            sems((3,)),
            sems((2, 2)), sems((2, 2)),
            sems((2, 7)), sems((2, 7)),
            sems((2, 7)), sems((2, 7)),
            sems((2, 8)), sems((2, 8)),
            sems((7, 4)), sems((7, 4)),
            sems((3,)), sems((3,)),
            sems((3,)), sems((3,)),
            sems((7, 4)), sems((7, 4)),
        ],
        compiler_params=pltpu.CompilerParams(
            collective_id=0, has_side_effects=True, vmem_limit_bytes=40 << 20
        ),
        name="soap",
    )(gradient, left_basis, right_basis, first_moment, second_moment)


def solution(mesh):
    placed = (
        P("row", "loop"),
        P("row", None),
        P("loop", "row"),
        P("loop", "row"),
        P("loop", "row"),
    )
    return jax.shard_map(
        per_device,
        mesh=mesh,
        in_specs=placed,
        out_specs=(P("row", "loop"), P("loop", "row"), P("loop", "row")),
        check_vma=False,
    )
```

time: 885 us -> 92.2 us (0.10)
  waiting for transfers between devices: 632 us -> 0 us
  blocking collectives: 227 us -> 0 us
  Pallas kernels: 0 us -> 84.1 us
  between operations: 14.1 us -> 0.65 us
    reduce_scatter x1 -> x0, waiting for transfers between devices: 632 us -> none  [per_device(): lax.psum_scatter(jnp.dot(rotated_half, right_basis, preferred_element_typ...]
    psum x2 -> x0, blocking collectives: 166 us -> none  [the longest x1 92.9 us: per_device(): back = lax.psum(back_part, 'row').astype(jnp.bfloat16)]
    pallas_call x0 -> x1, Pallas kernels: none -> 84.1 us  [per_device(): pl.pallas_call(kernel, out_shape=(jax.ShapeDtypeStruct((depth, width), BF...]
    all_gather x1 -> x0, blocking collectives: 61.6 us -> none  [per_device(): every_row = lax.all_gather(direction, 'loop', axis=0, tiled=True)]
  transfers between devices with their start and end apart: 1 -> 0, of which waited for: 1 -> 0; matrix products, arithmetic and copies ran while one was open for 0% -> 0% of each run, Pallas kernels for 0% -> 0%
where the time goes in v1:
time: 92.2 us; the launch traced here: 91.8 us
  Pallas kernels  84.1 us (91%)
  local copies, waits for them, and re-layouts  7.06 us (8%)
    pallas_call x1, Pallas kernels, per_device(): pl.pallas_call(kernel, out_shape=(jax.ShapeDtypeStruct((depth, width), BF...  84.1 us
    unnamed x13, local copies, waits for them, and re-layouts  7.06 us

profile of v1, /device:TPU:1, one launch (start us, length us, event | category | flops | bytes accessed | tf_op | source)
XLA Modules:
  0.0 91.8 jit_solution(4226770536443395289)
XLA Ops:
  0.6 0.0 copy-start
  0.6 1.2 %copy-done = bf16[512,896]{1,0:T(8,128)(2,1)S(1)} copy-done((bf16[512,896]{1,0:T(8,128)(2,1)S(1)}, bf16[512,896]{1,0:T(8,128)(2,1)}, u32[]{:S(2)}) %copy-start) | copy-done | bytes 917528
  1.8 0.0 copy-start.1
  1.8 1.2 %copy-done.1 = bf16[896,512]{1,0:T(8,128)(2,1)S(1)} copy-done((bf16[896,512]{1,0:T(8,128)(2,1)S(1)}, bf16[896,512]{1,0:T(8,128)(2,1)}, u32[]{:S(2)}) %copy-start.1) | copy-done | bytes 917528
  3.0 0.0 copy-start.2
  3.0 1.0 %copy-done.2 = bf16[512,512]{1,0:T(8,128)(2,1)S(1)} copy-done((bf16[512,512]{1,0:T(8,128)(2,1)S(1)}, bf16[512,512]{1,0:T(8,128)(2,1)}, u32[]{:S(2)}) %copy-start.2) | copy-done | bytes 524312
  4.0 0.0 copy-start.3
  4.0 0.8 copy-done.3
  4.8 0.0 copy-start.4
  4.8 0.8 copy-done.4
  5.5 84.1 %soap.1 = (bf16[512,896]{1,0:T(8,128)(2,1)S(1)}, f32[16,512]{1,0:T(8,128)S(1)}, f32[16,512]{1,0:T(8,128)S(1)}) custom-call(bf16[512,896]{1,0:T(8,128)(2,1)S(1)} %copy-done, bf16[512,512]{1,0:T(8,128)(2,1)S(1)} %copy-done.2, bf16[896,512]{1,0:T(8,128)(2,1)S(1)} %copy-done.1, f32[16,512]{1,0:T(8,128)S(1)} %copy-done.3, f32[16,512]{1,0:T(8,128)S(1)} %copy-done.4), custom_call_target="tpu_custom_call" | custom-call | tf_op jit(solution)/shard_map/soap/pallas_call | solution.py:272
  89.6 0.9 %copy.11 = bf16[512,896]{1,0:T(8,128)(2,1)} copy(bf16[512,896]{1,0:T(8,128)(2,1)S(1)} %get-tuple-element.6) | data formatting | bytes 1835008
  90.6 0.6 copy.12
  91.2 0.6 copy.13
Async XLA Ops:
  0.6 1.2 %copy-start = (bf16[512,896]{1,0:T(8,128)(2,1)S(1)}, bf16[512,896]{1,0:T(8,128)(2,1)}, u32[]{:S(2)}) copy-start(bf16[512,896]{1,0:T(8,128)(2,1)} %g_hbm.1) | copy-start | bytes 2752516
  1.8 1.2 %copy-start.1 = (bf16[896,512]{1,0:T(8,128)(2,1)S(1)}, bf16[896,512]{1,0:T(8,128)(2,1)}, u32[]{:S(2)}) copy-start(bf16[896,512]{1,0:T(8,128)(2,1)} %q_hbm.1) | copy-start | bytes 2752516
  3.0 1.0 %copy-start.2 = (bf16[512,512]{1,0:T(8,128)(2,1)S(1)}, bf16[512,512]{1,0:T(8,128)(2,1)}, u32[]{:S(2)}) copy-start(bf16[512,512]{1,0:T(8,128)(2,1)} %l_hbm.1) | copy-start | bytes 1572868
  4.0 0.8 copy-start.3
  4.8 0.8 copy-start.4

commit v2 on v0

v2 whole, which is shorter than its diff:
```python
import functools

import jax
import jax.numpy as jnp
from jax import lax
from jax.experimental import pallas as pl
from jax.experimental.pallas import tpu as pltpu
from jax.sharding import PartitionSpec as P

MESH = pl.DeviceIdType.MESH
BF16 = jnp.bfloat16
F32 = jnp.float32
RING = 16
QUAD = 4


def dot(a, b):
    return jnp.dot(a, b, preferred_element_type=F32)


def kernel(
    g_hbm, l_hbm, q_hbm, m1_hbm, m2_hbm,
    back_hbm, left_hbm, projected_ref,
    g, lb, q, m1, m2, lt, lp, qt,
    xs, xr, hs, rr, keep, full,
    own, ps, bq, near, bs, br, dirp, dirf,
    in_sem, out_sem, core_s, core_r, sum_s, sum_r, all_s, all_r, relay_s, relay_r,
    near_s, near_r, far_s, far_r, dfar_s, dfar_r, dnear_s, dnear_r,
):
    row, loop = lax.axis_index("row"), lax.axis_index("loop")
    core, x, y = row % 2, (row // 2) % 2, row // 4
    here, z = loop // RING, loop % RING
    there = 1 - here
    chip = y * 2 + x
    offsets = (2 - 4 * core, 1, -1)
    partners = [(there, o) for o in offsets] + [(there, 0)] + [(here, o) for o in offsets]
    sibling = (row + 1 - 2 * core, loop)

    loads = [
        pltpu.make_async_copy(src, dst, in_sem.at[n])
        for n, (src, dst) in enumerate(
            ((l_hbm, lb), (g_hbm, g), (q_hbm, q), (m1_hbm, m1), (m2_hbm, m2))
        )
    ]
    for load in loads:
        load.start()

    def chip_of(m):
        py = y
        if m & 2:
            py = py + 1 - 2 * (py % 2)
        if m & 4:
            py = (py + 2) % 4
        px = 1 - x if m & 1 else x
        return py * 2 + px

    def in_row(m):
        return (chip_of(m) * 2 + core, loop)

    def moved(o):
        return (z + o + RING) % RING

    def at(plane, o):
        return (row, plane * RING + moved(o))

    barrier = pltpu.get_barrier_semaphore()
    senders = [at(here, QUAD * t) for t in (2, 1, 3)] + [at(plane, -o) for plane, o in partners]
    senders += [in_row(m) for m in range(1, 8)] + [sibling]
    for device in senders:
        pl.semaphore_signal(barrier, inc=1, device_id=device, device_id_type=MESH)

    loads[0].wait()
    lb[...] = lb[...].T
    for plane in range(2):
        for s in range(QUAD):
            for a in range(0, QUAD, 2):
                two = [
                    lb[16 * (plane * RING + i * QUAD + s) : 16 * (plane * RING + i * QUAD + s + 1), :].astype(F32)
                    for i in (a, a + 1)
                ]
                for c in range(2):
                    dst = 256 * c + 128 * plane + 32 * s + 8 * a
                    lt[dst : dst + 16, :] = jnp.concatenate(
                        [v[8 * c : 8 * c + 8] for v in two], axis=0
                    ).astype(BF16)
    loads[1].wait()

    sent = []

    def send(src, dst, s_sem, r_sem, device):
        copy = pltpu.make_async_remote_copy(
            src_ref=src, dst_ref=dst, send_sem=s_sem, recv_sem=r_sem,
            device_id=device, device_id_type=MESH,
        )
        copy.start()
        sent.append(copy)

    def landing(dst, s_sem, r_sem):
        pltpu.make_async_remote_copy(
            src_ref=dst, dst_ref=dst, send_sem=s_sem, recv_sem=r_sem,
            device_id=sibling, device_id_type=MESH,
        ).wait_recv()

    def rows(start, count):
        return pl.ds(pl.multiple_of(start, count), count)

    def packed(value):
        n, w = value.shape[0] // 8, value.shape[1] // 2
        value = value.reshape(n, 8, 2 * w)
        return jnp.concatenate([value[:, :, :w], value[:, :, w:]], axis=1).reshape(16 * n, w)

    def unpacked(value):
        n, w = value.shape[0] // 16, value.shape[1]
        value = value.reshape(n, 16, w)
        return jnp.concatenate([value[:, :8], value[:, 8:]], axis=2).reshape(8 * n, 2 * w)

    def row_sum(turn, c, part):
        i = 2 * turn + c
        xs[i] = part(128 * (1 - core)).astype(BF16)
        if i == 0:
            pl.semaphore_wait(barrier, len(senders))
        send(xs.at[i], xr.at[i], core_s.at[i], core_r.at[i], sibling)
        yield
        mine = part(128 * core)
        landing(xr.at[i], core_s.at[i], core_r.at[i])
        both = mine + xr[i].astype(F32)
        hs[i] = both.astype(BF16)
        keep[i] = both
        for m in (5, 4, 7, 3, 6, 2, 1):
            send(
                hs.at[i, rows(16 * chip_of(m), 16)], rr.at[i, m - 1],
                sum_s.at[i, m - 1], sum_r.at[i, m - 1], in_row(m),
            )
        yield
        total = keep[i, rows(16 * chip, 16), :]
        for m in (1, 2, 6, 3, 7, 4, 5):
            landing(rr.at[i, m - 1], sum_s.at[i, m - 1], sum_r.at[i, m - 1])
            total = total + rr[i, m - 1].astype(F32)

        def piece(half, m):
            return full.at[turn, rows(256 * c + 128 * half + 16 * chip_of(m), 16)]

        own_piece = piece(core, 0)
        own_piece[...] = total.astype(BF16)
        for m in (5, 4, 7, 3, 6, 2, 1):
            send(own_piece, own_piece, all_s.at[i, m - 1], all_r.at[i, m - 1], in_row(m))
        send(own_piece, own_piece, relay_s.at[i, 0], relay_r.at[i, 0], sibling)
        yield
        for m in (1, 2, 6, 3, 7, 4, 5):
            landing(piece(core, m), all_s.at[i, m - 1], all_r.at[i, m - 1])
            send(piece(core, m), piece(core, m), relay_s.at[i, m], relay_r.at[i, m], sibling)
        for m in range(8):
            landing(piece(1 - core, m), relay_s.at[i, m], relay_r.at[i, m])

    def chunk(c):
        yield from row_sum(
            0, c, lambda r: dot(lt[pl.ds(pl.multiple_of(256 * c + r, 128), 128), :], g[...])
        )

        value = packed(dot(full[0, 256 * c : 256 * c + 256, :], q[...]))
        own[c] = value
        ps[c] = value.astype(BF16)
        for n, (plane, o) in enumerate(partners):
            send(
                ps.at[c, rows(64 * (plane * QUAD + moved(o) % QUAD), 64)], bq.at[c, n],
                near_s.at[c, n], near_r.at[c, n], at(plane, o),
            )
        yield
        total = own[c, rows(64 * (here * QUAD + z % QUAD), 64), :]
        for n in (4, 5, 6, 3, 1, 2, 0):
            landing(bq.at[c, n], near_s.at[c, n], near_r.at[c, n])
            total = total + bq[c, n].astype(F32)
        near[c] = total
        bs[c] = total.astype(BF16)
        for t in (2, 1, 3):
            send(
                bs.at[c, rows(16 * ((z // QUAD + t) % QUAD), 16)], br.at[c, t - 1],
                far_s.at[c, t - 1], far_r.at[c, t - 1], at(here, QUAD * t),
            )
        yield
        total = near[c, rows(16 * (z // QUAD), 16), :]
        for t in (1, 3, 2):
            landing(br.at[c, t - 1], far_s.at[c, t - 1], far_r.at[c, t - 1])
            total = total + br[c, t - 1].astype(F32)
        total = unpacked(total)
        mine = slice(8 * c, 8 * c + 8)
        projected_ref[mine, :] = total
        first = 0.9 * m1[mine, :] + 0.1 * total
        second = 0.95 * m2[mine, :] + 0.05 * total * total

        def slice_of(plane, o):
            zz = moved(o)
            return dirp.at[c, rows(16 * (plane * RING + (zz % QUAD) * QUAD + zz // QUAD), 16)]

        piece = slice_of(here, 0)
        piece[...] = packed(first / (jnp.sqrt(second) + 1e-08)).astype(BF16)
        for t in (2, 1, 3):
            send(piece, piece, dfar_s.at[c, t - 1], dfar_r.at[c, t - 1], at(here, QUAD * t))

        def forward(t):
            piece = slice_of(here, -QUAD * t)
            for n, (plane, o) in enumerate(partners):
                send(piece, piece, dnear_s.at[c, n, t], dnear_r.at[c, n, t], at(plane, o))

        forward(0)
        yield
        for t in (1, 3, 2):
            landing(slice_of(here, -QUAD * t), dfar_s.at[c, t - 1], dfar_r.at[c, t - 1])
            forward(t)
        yield
        for t in (0, 1, 3, 2):
            for n, (plane, o) in enumerate(partners):
                landing(slice_of(plane, -o - QUAD * t), dnear_s.at[c, n, t], dnear_r.at[c, n, t])
        dirf[c] = unpacked(dirp[c].astype(F32)).astype(BF16)
        yield from row_sum(1, c, lambda r: dot(dirf[c, rows(r, 128), :], qt[...]))
        done = pltpu.make_async_copy(
            full.at[1, pl.ds(256 * c, 256)], back_hbm.at[pl.ds(256 * c, 256)], out_sem.at[c]
        )
        done.start()
        finals.append(done)

    finals = []
    chunks = [chunk(0), chunk(1)]
    step = 0
    while chunks:
        for each in list(chunks):
            if next(each, finals) is finals:
                chunks.remove(each)
        step += 1
        if step == 2:
            loads[2].wait()
            qt[...] = q[...].T
        if step == 3:
            lp[...] = lt[...].T
            left = pltpu.make_async_copy(lp, left_hbm, out_sem.at[2])
            left.start()
            finals.append(left)
            loads[3].wait()
            loads[4].wait()
    for copy in sent:
        copy.wait_send()
    for copy in finals:
        copy.wait()


def finish(left_ref, back_ref, projected_ref, m1_ref, m2_ref, update_ref, first_ref, second_ref):
    projected = projected_ref[...]
    first_ref[...] = 0.9 * m1_ref[...] + 0.1 * projected
    second_ref[...] = 0.95 * m2_ref[...] + 0.05 * projected * projected
    update_ref[...] = dot(left_ref[...], back_ref[...]).astype(BF16)


def per_device(gradient, left_basis, right_basis, first_moment, second_moment):
    depth, width = gradient.shape
    window = left_basis.shape[1]
    cols = right_basis.shape[1]
    mine = first_moment.shape[0]
    sems = pltpu.SemaphoreType.DMA
    back, left, projected = pl.pallas_call(
        kernel,
        out_shape=(
            jax.ShapeDtypeStruct((window, width), BF16),
            jax.ShapeDtypeStruct((depth, window), BF16),
            jax.ShapeDtypeStruct((mine, cols), F32),
        ),
        in_specs=[pl.BlockSpec(memory_space=pl.ANY)] * 5,
        out_specs=[pl.BlockSpec(memory_space=pl.ANY)] * 2 + [pl.BlockSpec(memory_space=pltpu.VMEM)],
        scratch_shapes=[
            pltpu.VMEM((depth, width), BF16),
            pltpu.VMEM((depth, window), BF16),
            pltpu.VMEM((width, cols), BF16),
            pltpu.VMEM((mine, cols), F32),
            pltpu.VMEM((mine, cols), F32),
            pltpu.VMEM((window, depth), BF16),
            pltpu.VMEM((depth, window), BF16),
            pltpu.VMEM((cols, width), BF16),
            pltpu.VMEM((4, 128, width), BF16),
            pltpu.VMEM((4, 128, width), BF16),
            pltpu.VMEM((4, 128, width), BF16),
            pltpu.VMEM((4, 7, 16, width), BF16),
            pltpu.VMEM((4, 128, width), F32),
            pltpu.VMEM((2, window, width), BF16),
            pltpu.VMEM((2, window, cols // 2), F32),
            pltpu.VMEM((2, window, cols // 2), BF16),
            pltpu.VMEM((2, 7, 64, cols // 2), BF16),
            pltpu.VMEM((2, 64, cols // 2), F32),
            pltpu.VMEM((2, 64, cols // 2), BF16),
            pltpu.VMEM((2, 3, mine, cols // 2), BF16),
            pltpu.VMEM((2, window, cols // 2), BF16),
            pltpu.VMEM((2, window // 2, cols), BF16),
            sems((5,)), sems((3,)),
            sems((4,)), sems((4,)),
            sems((4, 7)), sems((4, 7)),
            sems((4, 7)), sems((4, 7)),
            sems((4, 8)), sems((4, 8)),
            sems((2, 7)), sems((2, 7)),
            sems((2, 3)), sems((2, 3)),
            sems((2, 3)), sems((2, 3)),
            sems((2, 7, 4)), sems((2, 7, 4)),
        ],
        compiler_params=pltpu.CompilerParams(
            collective_id=0, has_side_effects=True, vmem_limit_bytes=60 << 20
        ),
        name="soap",
    )(gradient, left_basis, right_basis, first_moment, second_moment)
    block = 128
    small = pl.BlockSpec((mine, cols), lambda i: (0, 0))
    return pl.pallas_call(
        finish,
        grid=(depth // block,),
        out_shape=(
            jax.ShapeDtypeStruct((depth, width), BF16),
            jax.ShapeDtypeStruct(first_moment.shape, F32),
            jax.ShapeDtypeStruct(second_moment.shape, F32),
        ),
        in_specs=[
            pl.BlockSpec((block, window), lambda i: (i, 0)),
            pl.BlockSpec((window, width), lambda i: (0, 0)),
            small, small, small,
        ],
        out_specs=[pl.BlockSpec((block, width), lambda i: (i, 0)), small, small],
        compiler_params=pltpu.CompilerParams(vmem_limit_bytes=60 << 20),
        name="finish",
    )(left, back, projected, first_moment, second_moment)


def solution(mesh):
    placed = (
        P("row", "loop"),
        P("row", None),
        P("loop", "row"),
        P("loop", "row"),
        P("loop", "row"),
    )
    return jax.shard_map(
        per_device,
        mesh=mesh,
        in_specs=placed,
        out_specs=(P("row", "loop"), P("loop", "row"), P("loop", "row")),
        check_vma=False,
    )
```

time: 885 us -> 83.2 us (0.09)
  waiting for transfers between devices: 632 us -> 0 us
  blocking collectives: 227 us -> 0 us
  Pallas kernels: 0 us -> 82.4 us
  between operations: 14.1 us -> 0.64 us
    reduce_scatter x1 -> x0, waiting for transfers between devices: 632 us -> none  [per_device(): lax.psum_scatter(jnp.dot(rotated_half, right_basis, preferred_element_typ...]
    psum x2 -> x0, blocking collectives: 166 us -> none  [the longest x1 92.9 us: per_device(): back = lax.psum(back_part, 'row').astype(jnp.bfloat16)]
    pallas_call x0 -> x2, Pallas kernels: none -> 82.4 us  [the longest x1 78.1 us: per_device(): pl.pallas_call(kernel, out_shape=(jax.ShapeDtypeStruct((window, width), B...]
    all_gather x1 -> x0, blocking collectives: 61.6 us -> none  [per_device(): every_row = lax.all_gather(direction, 'loop', axis=0, tiled=True)]
  transfers between devices with their start and end apart: 1 -> 0, of which waited for: 1 -> 0; matrix products, arithmetic and copies ran while one was open for 0% -> 0% of each run, Pallas kernels for 0% -> 0%
where the time goes in v2:
time: 83.2 us; the launch traced here: 83 us
  Pallas kernels  82.4 us (99%)
    pallas_call x1, Pallas kernels, per_device(): pl.pallas_call(kernel, out_shape=(jax.ShapeDtypeStruct((window, width), B...  78.1 us
    pallas_call x1, Pallas kernels, per_device(): pl.pallas_call(finish, grid=(depth // block,), out_shape=(jax.ShapeDtypeS...  4.23 us

profile of v2, /device:TPU:1, one launch (start us, length us, event | category | flops | bytes accessed | tf_op | source)
XLA Modules:
  0.0 83.0 jit_solution(18028127560403462607)
XLA Ops:
  0.6 78.1 %soap.1 = (bf16[512,896]{1,0:T(8,128)(2,1)}, bf16[512,512]{1,0:T(8,128)(2,1)}, f32[16,512]{1,0:T(8,128)}) custom-call(bf16[512,896]{1,0:T(8,128)(2,1)} %g_hbm.1, bf16[512,512]{1,0:T(8,128)(2,1)} %l_hbm.1, bf16[896,512]{1,0:T(8,128)(2,1)} %q_hbm.1, f32[16,512]{1,0:T(8,128)} %m1_ref.1, f32[16,512]{1,0:T(8,128)} %m2_ref.1), custom_call_target="tpu_custom_call" | custom-call | tf_op jit(solution)/shard_map/soap/pallas_call | solution.py:259
  78.8 4.2 %finish.1 = (bf16[512,896]{1,0:T(8,128)(2,1)}, f32[16,512]{1,0:T(8,128)}, f32[16,512]{1,0:T(8,128)}) custom-call(bf16[512,512]{1,0:T(8,128)(2,1)} %get-tuple-element.6.left_ref, bf16[512,896]{1,0:T(8,128)(2,1)} %get-tuple-element.7.back_ref, f32[16,512]{1,0:T(8,128)} %get-tuple-element.8.projected_ref, f32[16,512]{1,0:T(8,128)} %m1_ref.1, f32[16,512]{1,0:T(8,128)} %m2_ref.1), custom_call_target="tpu_custom_call" | custom-call | tf_op jit(solution)/shard_map/finish/pallas_call | solution.py:308

commit v3 on v2

--- a/solution.py
+++ b/solution.py
@@ -25,7 +25,7 @@
     xs, xr, hs, rr, keep, full,
     own, ps, bq, near, bs, br, dirp, dirf,
     in_sem, out_sem, core_s, core_r, sum_s, sum_r, all_s, all_r, relay_s, relay_r,
-    near_s, near_r, far_s, far_r, dfar_s, dfar_r, dnear_s, dnear_r,
+    near_s, near_r, far_s, far_r, dfar_s, dfar_r, dnear_s, dnear_r, met,
 ):
     row, loop = lax.axis_index("row"), lax.axis_index("loop")
     core, x, y = row % 2, (row // 2) % 2, row // 4
@@ -64,10 +64,13 @@
         return (row, plane * RING + moved(o))
 
     barrier = pltpu.get_barrier_semaphore()
-    senders = [at(here, QUAD * t) for t in (2, 1, 3)] + [at(plane, -o) for plane, o in partners]
-    senders += [in_row(m) for m in range(1, 8)] + [sibling]
-    for device in senders:
-        pl.semaphore_signal(barrier, inc=1, device_id=device, device_id_type=MESH)
+    greeted = [at(here, 1), at(here, -1), at(there, 0)] + [in_row(m) for m in range(1, 8)] + [sibling]
+
+    def greet(sem, devices):
+        for device in devices:
+            pl.semaphore_signal(sem, inc=1, device_id=device, device_id_type=MESH)
+
+    greet(barrier, greeted)
 
     loads[0].wait()
     lb[...] = lb[...].T
@@ -118,7 +121,8 @@
         i = 2 * turn + c
         xs[i] = part(128 * (1 - core)).astype(BF16)
         if i == 0:
-            pl.semaphore_wait(barrier, len(senders))
+            pl.semaphore_wait(barrier, len(greeted))
+            greet(met.at[0], [at(here, 1), at(here, -1)])
         send(xs.at[i], xr.at[i], core_s.at[i], core_r.at[i], sibling)
         yield
         mine = part(128 * core)
@@ -160,6 +164,8 @@
         value = packed(dot(full[0, 256 * c : 256 * c + 256, :], q[...]))
         own[c] = value
         ps[c] = value.astype(BF16)
+        if c == 0:
+            pl.semaphore_wait(met.at[3], 1)
         for n, (plane, o) in enumerate(partners):
             send(
                 ps.at[c, rows(64 * (plane * QUAD + moved(o) % QUAD), 64)], bq.at[c, n],
@@ -172,6 +178,8 @@
             total = total + bq[c, n].astype(F32)
         near[c] = total
         bs[c] = total.astype(BF16)
+        if c == 0:
+            pl.semaphore_wait(met.at[2], 2)
         for t in (2, 1, 3):
             send(
                 bs.at[c, rows(16 * ((z // QUAD + t) % QUAD), 16)], br.at[c, t - 1],
@@ -230,6 +238,9 @@
         if step == 2:
             loads[2].wait()
             qt[...] = q[...].T
+            pl.semaphore_wait(met.at[0], 2)
+            greet(met.at[1], [at(here, 2), at(here, -2)])
+            greet(met.at[3], [at(there, 0)])
         if step == 3:
             lp[...] = lt[...].T
             left = pltpu.make_async_copy(lp, left_hbm, out_sem.at[2])
@@ -237,17 +248,49 @@
             finals.append(left)
             loads[3].wait()
             loads[4].wait()
+            pl.semaphore_wait(met.at[1], 2)
+            greet(met.at[2], [at(here, 4), at(here, -4)])
     for copy in sent:
         copy.wait_send()
     for copy in finals:
         copy.wait()
 
 
-def finish(left_ref, back_ref, projected_ref, m1_ref, m2_ref, update_ref, first_ref, second_ref):
-    projected = projected_ref[...]
-    first_ref[...] = 0.9 * m1_ref[...] + 0.1 * projected
-    second_ref[...] = 0.95 * m2_ref[...] + 0.05 * projected * projected
-    update_ref[...] = dot(left_ref[...], back_ref[...]).astype(BF16)
+def finish(
+    left_hbm, back_hbm, projected_hbm, m1_hbm, m2_hbm, update_hbm, first_hbm, second_hbm,
+    left, back, projected, m1, m2, update, in_sem, out_sem,
+):
+    half = back.shape[0] // 2
+    pairs = (
+        (left_hbm, left),
+        (back_hbm.at[pl.ds(0, half)], back.at[pl.ds(0, half)]),
+        (back_hbm.at[pl.ds(half, half)], back.at[pl.ds(half, half)]),
+        (projected_hbm, projected), (m1_hbm, m1), (m2_hbm, m2),
+    )
+    loads = [pltpu.make_async_copy(src, dst, in_sem.at[n]) for n, (src, dst) in enumerate(pairs)]
+    for load in loads:
+        load.start()
+    for load in loads[3:]:
+        load.wait()
+    value = projected[...]
+    m1[...] = 0.9 * m1[...] + 0.1 * value
+    m2[...] = 0.95 * m2[...] + 0.05 * value * value
+    stores = [
+        pltpu.make_async_copy(m1, first_hbm, out_sem.at[0]),
+        pltpu.make_async_copy(m2, second_hbm, out_sem.at[1]),
+    ]
+    for store in stores:
+        store.start()
+    for load in loads[:3]:
+        load.wait()
+    for n in range(4):
+        block = pl.ds(128 * n, 128)
+        update[block, :] = dot(left[block, :], back[...]).astype(BF16)
+        store = pltpu.make_async_copy(update.at[block], update_hbm.at[block], out_sem.at[2 + n])
+        store.start()
+        stores.append(store)
+    for store in stores:
+        store.wait()
 
 
 def per_device(gradient, left_basis, right_basis, first_moment, second_moment):
@@ -297,28 +340,31 @@
             sems((2, 3)), sems((2, 3)),
             sems((2, 3)), sems((2, 3)),
             sems((2, 7, 4)), sems((2, 7, 4)),
+            pltpu.SemaphoreType.REGULAR((4,)),
         ],
         compiler_params=pltpu.CompilerParams(
             collective_id=0, has_side_effects=True, vmem_limit_bytes=60 << 20
         ),
         name="soap",
     )(gradient, left_basis, right_basis, first_moment, second_moment)
-    block = 128
-    small = pl.BlockSpec((mine, cols), lambda i: (0, 0))
     return pl.pallas_call(
         finish,
-        grid=(depth // block,),
         out_shape=(
             jax.ShapeDtypeStruct((depth, width), BF16),
             jax.ShapeDtypeStruct(first_moment.shape, F32),
             jax.ShapeDtypeStruct(second_moment.shape, F32),
         ),
-        in_specs=[
-            pl.BlockSpec((block, window), lambda i: (i, 0)),
-            pl.BlockSpec((window, width), lambda i: (0, 0)),
-            small, small, small,
+        in_specs=[pl.BlockSpec(memory_space=pl.ANY)] * 5,
+        out_specs=[pl.BlockSpec(memory_space=pl.ANY)] * 3,
+        scratch_shapes=[
+            pltpu.VMEM((depth, window), BF16),
+            pltpu.VMEM((window, width), BF16),
+            pltpu.VMEM((mine, cols), F32),
+            pltpu.VMEM((mine, cols), F32),
+            pltpu.VMEM((mine, cols), F32),
+            pltpu.VMEM((depth, width), BF16),
+            sems((6,)), sems((6,)),
         ],
-        out_specs=[pl.BlockSpec((block, width), lambda i: (i, 0)), small, small],
         compiler_params=pltpu.CompilerParams(vmem_limit_bytes=60 << 20),
         name="finish",
     )(left, back, projected, first_moment, second_moment)

time: 83.2 us -> 78.1 us (0.939)
  Pallas kernels: 82.4 us -> 77.3 us
    pallas_call x1, Pallas kernels: 78.1 us -> 74.5 us  [per_device(): pl.pallas_call(kernel, out_shape=(jax.ShapeDtypeStruct((window, width), B...]
    pallas_call x1, Pallas kernels: 4.23 us -> 2.83 us  [per_device(): pl.pallas_call(finish, out_shape=(jax.ShapeDtypeStruct((depth, width), BF...]
where the time goes in v3:
time: 78.1 us; the launch traced here: 77.9 us
  Pallas kernels  77.3 us (99%)
    pallas_call x1, Pallas kernels, per_device(): pl.pallas_call(kernel, out_shape=(jax.ShapeDtypeStruct((window, width), B...  74.5 us
    pallas_call x1, Pallas kernels, per_device(): pl.pallas_call(finish, out_shape=(jax.ShapeDtypeStruct((depth, width), BF...  2.83 us

profile of v3, /device:TPU:1, one launch (start us, length us, event | category | flops | bytes accessed | tf_op | source)
XLA Modules:
  0.0 77.9 jit_solution(8439774236515646270)
XLA Ops:
  0.6 74.5 %soap.1 = (bf16[512,896]{1,0:T(8,128)(2,1)}, bf16[512,512]{1,0:T(8,128)(2,1)}, f32[16,512]{1,0:T(8,128)}) custom-call(bf16[512,896]{1,0:T(8,128)(2,1)} %g_hbm.1, bf16[512,512]{1,0:T(8,128)(2,1)} %l_hbm.1, bf16[896,512]{1,0:T(8,128)(2,1)} %q_hbm.1, f32[16,512]{1,0:T(8,128)} %m1_hbm.3, f32[16,512]{1,0:T(8,128)} %m2_hbm.3), custom_call_target="tpu_custom_call" | custom-call | tf_op jit(solution)/shard_map/soap/pallas_call | solution.py:302
  75.1 2.8 %finish.1 = (bf16[512,896]{1,0:T(8,128)(2,1)}, f32[16,512]{1,0:T(8,128)}, f32[16,512]{1,0:T(8,128)}) custom-call(bf16[512,512]{1,0:T(8,128)(2,1)} %get-tuple-element.6.left_hbm, bf16[512,896]{1,0:T(8,128)(2,1)} %get-tuple-element.7.back_hbm, f32[16,512]{1,0:T(8,128)} %get-tuple-element.8.projected_hbm, f32[16,512]{1,0:T(8,128)} %m1_hbm.3, f32[16,512]{1,0:T(8,128)} %m2_hbm.3), custom_call_target="tpu_custom_call" | custom-call | tf_op jit(solution)/shard_map/finish/pallas_call | solution.py:350

commit v4 on v3

--- a/solution.py
+++ b/solution.py
@@ -130,7 +130,7 @@
         both = mine + xr[i].astype(F32)
         hs[i] = both.astype(BF16)
         keep[i] = both
-        for m in (5, 4, 7, 3, 6, 2, 1):
+        for m in (3, 5, 7, 4, 2, 6, 1):
             send(
                 hs.at[i, rows(16 * chip_of(m), 16)], rr.at[i, m - 1],
                 sum_s.at[i, m - 1], sum_r.at[i, m - 1], in_row(m),
@@ -146,7 +146,7 @@
 
         own_piece = piece(core, 0)
         own_piece[...] = total.astype(BF16)
-        for m in (5, 4, 7, 3, 6, 2, 1):
+        for m in (3, 5, 7, 4, 2, 6, 1):
             send(own_piece, own_piece, all_s.at[i, m - 1], all_r.at[i, m - 1], in_row(m))
         send(own_piece, own_piece, relay_s.at[i, 0], relay_r.at[i, 0], sibling)
         yield
@@ -228,6 +228,14 @@
         finals.append(done)
 
     finals = []
+    marks = []
+    settled = [0]
+
+    def settle(count):
+        for copy in sent[settled[0] : count]:
+            copy.wait_send()
+        settled[0] = count
+
     chunks = [chunk(0), chunk(1)]
     step = 0
     while chunks:
@@ -235,6 +243,9 @@
             if next(each, finals) is finals:
                 chunks.remove(each)
         step += 1
+        marks.append(len(sent))
+        if step > 2:
+            settle(marks[step - 3])
         if step == 2:
             loads[2].wait()
             qt[...] = q[...].T
@@ -250,8 +261,7 @@
             loads[4].wait()
             pl.semaphore_wait(met.at[1], 2)
             greet(met.at[2], [at(here, 4), at(here, -4)])
-    for copy in sent:
-        copy.wait_send()
+    settle(len(sent))
     for copy in finals:
         copy.wait()
 

time: 78.1 us -> 77.5 us (level)
  no operation moved by 1% of the time
where the time goes in v4:
time: 77.5 us; the launch traced here: 77.4 us
  Pallas kernels  76.7 us (99%)
    pallas_call x1, Pallas kernels, per_device(): pl.pallas_call(kernel, out_shape=(jax.ShapeDtypeStruct((window, width), B...  73.9 us
    pallas_call x1, Pallas kernels, per_device(): pl.pallas_call(finish, out_shape=(jax.ShapeDtypeStruct((depth, width), BF...  2.84 us

profile of v4, /device:TPU:1, one launch (start us, length us, event | category | flops | bytes accessed | tf_op | source)
XLA Modules:
  0.0 77.4 jit_solution(16054650416487846453)
XLA Ops:
  0.6 73.9 %soap.1 = (bf16[512,896]{1,0:T(8,128)(2,1)}, bf16[512,512]{1,0:T(8,128)(2,1)}, f32[16,512]{1,0:T(8,128)}) custom-call(bf16[512,896]{1,0:T(8,128)(2,1)} %g_hbm.1, bf16[512,512]{1,0:T(8,128)(2,1)} %l_hbm.1, bf16[896,512]{1,0:T(8,128)(2,1)} %q_hbm.1, f32[16,512]{1,0:T(8,128)} %m1_hbm.3, f32[16,512]{1,0:T(8,128)} %m2_hbm.3), custom_call_target="tpu_custom_call" | custom-call | tf_op jit(solution)/shard_map/soap/pallas_call | solution.py:312
  74.5 2.8 %finish.1 = (bf16[512,896]{1,0:T(8,128)(2,1)}, f32[16,512]{1,0:T(8,128)}, f32[16,512]{1,0:T(8,128)}) custom-call(bf16[512,512]{1,0:T(8,128)(2,1)} %get-tuple-element.6.left_hbm, bf16[512,896]{1,0:T(8,128)(2,1)} %get-tuple-element.7.back_hbm, f32[16,512]{1,0:T(8,128)} %get-tuple-element.8.projected_hbm, f32[16,512]{1,0:T(8,128)} %m1_hbm.3, f32[16,512]{1,0:T(8,128)} %m2_hbm.3), custom_call_target="tpu_custom_call" | custom-call | tf_op jit(solution)/shard_map/finish/pallas_call | solution.py:360
